TPU v7x, 32 devices: a whole 2x2x4 slice. The times are simulated.
32 devices in a mesh: amp: 8 (over z, x), int: 4 (over y, core).
Axes of the slice: x: 2, y: 2, z: 4, core: 2. Of those that a mesh axis runs over, the one named last changes fastest.
Arguments:
- t2_stored: float32 [1024, 4096], P('amp', 'int'), may hold values from -6 to 6
- integrals: float32 [4096, 4096], P('amp', 'int'), may hold values from -0.09375 to 0.09375
- driver: float32 [1024, 4096], P('amp', 'int'), may hold values from -6 to 6
- eps_occ: float32 [120], replicated, may hold values from -2 to -0.3
- eps_vir: float32 [600], replicated, may hold values from 0.1 to 3
- blk_len: int32 [32], replicated, may hold values from 32 to 128, as said below
- t2_order: int32 [32], replicated, may hold values from 0 to 31, as said below
- int_order: int32 [32], replicated, may hold values from 0 to 31, as said below
Outputs:
- update: float32 [1024, 4096], P('amp', 'int')
Inputs may be any that keep to these rules, and one draw needn't show every extreme that they name: `blk_len`: live slots of a block come first; some block is full and some has 32 live slots. `int_order`: a permutation of the blocks; the integrals' row blocks on one amp index are int_order's blocks of that index. `t2_order`: a permutation of the blocks; the stored column blocks on each int index hold exactly one of the blocks that int_order places on each amp index.
All inputs are finite; a program needn't handle non-finite values.
Results may differ from a plain program's by a relative error of at most 0.00005.
Values sent between devices are 32-bit elements; how exact they have to be, the bound alone decides.
A program may use at most 128 MiB of HBM per device.

v0:
```python
import jax
import jax.numpy as jnp
from jax import lax
from jax.sharding import PartitionSpec as P

NO = 120
NV = 600
TILE = 128


def inverse_of(perm, counter):
    return jnp.sum(jnp.where(perm[None, :] == counter[:, None], counter[None, :], 0), axis=1)


def lookup(table, indices):
    places = jnp.arange(table.shape[0], dtype=jnp.int32)
    return jnp.sum(
        jnp.where(indices[:, None] == places[None, :], table[None, :], jnp.float32(0.0)), axis=1
    )


def on_device(t2_stored, integrals, driver, eps_occ, eps_vir, blk_len, t2_order, int_order):
    row_count = t2_stored.shape[0]
    col_count = integrals.shape[1]
    block_count = blk_len.shape[0]
    owned = integrals.shape[0] // TILE
    per_slice = t2_stored.shape[1] // TILE
    amp_place = lax.axis_index("amp")
    int_place = lax.axis_index("int")
    counter = jnp.arange(block_count, dtype=jnp.int32)
    live_mask = (jnp.arange(TILE, dtype=jnp.int32)[None, :] < blk_len[:, None]).astype(jnp.float32)
    inverse_t2 = inverse_of(t2_order, counter)
    my_blocks = lax.dynamic_slice_in_dim(int_order, amp_place * owned, owned)
    source_block = jnp.take(inverse_t2, my_blocks)
    holder = source_block // per_slice
    all_rows = lax.all_gather(t2_stored, "amp", axis=0, tiled=True)
    here = holder == int_place
    local_pick = jnp.sum(jnp.where(here, source_block % per_slice, 0))
    logical_pick = jnp.sum(jnp.where(here, my_blocks, 0))
    live_row = lax.dynamic_slice_in_dim(live_mask, logical_pick, 1, 0)
    piece = lax.dynamic_slice_in_dim(all_rows, local_pick * TILE, TILE, 1) * live_row
    collected = lax.all_gather(piece, "int", axis=1, tiled=True)
    stacked = collected.reshape(collected.shape[0], owned, TILE)
    amplitudes = jnp.take(stacked, holder, axis=1).reshape(collected.shape[0], owned * TILE)
    summed = lax.psum_scatter(
        jnp.dot(
            amplitudes,
            integrals,
            precision=lax.Precision.HIGHEST,
            preferred_element_type=jnp.float32,
        ),
        "amp",
        scatter_dimension=0,
        tiled=True,
    )
    residual = driver + summed
    row_ids = amp_place * row_count + jnp.arange(row_count, dtype=jnp.int32)
    col_ids = int_place * col_count + jnp.arange(col_count, dtype=jnp.int32)
    occ_first = lookup(eps_occ, row_ids // NO)
    occ_second = lookup(eps_occ, row_ids % NO)
    vir_first = lookup(eps_vir, col_ids % NV)
    vir_second = lookup(eps_vir, (3 * col_ids + col_ids // NV) % NV)
    denominators = (
        vir_first[None, :] + vir_second[None, :] - occ_first[:, None] - occ_second[:, None]
    )
    live_cols = lax.dynamic_slice_in_dim(
        live_mask.reshape(block_count * TILE), int_place * col_count, col_count
    )
    return residual * live_cols[None, :] / denominators


def solution(mesh):
    placed = (P("amp", "int"), P("amp", "int"), P("amp", "int"), P(), P(), P(), P(), P())
    return jax.shard_map(
        on_device, mesh=mesh, in_specs=placed, out_specs=P("amp", "int"), check_vma=False
    )
```

profile of v0, /device:TPU:0, one launch (start us, length us, event | category | flops | bytes accessed | tf_op | source)
XLA Modules:
  0.0 226.4 jit_solution(14133576417330878228)
XLA Ops:
  6.5 0.0 copy-start
  6.5 0.0 all-gather.3.cloned.1.call-start
  6.5 2.2 copy.12
  8.7 0.0 all-gather.3.cloned.1.call-update
  8.8 0.0 all-gather.5.cloned.1.call-start
  8.8 0.7 compare_select_fusion.1
  9.6 0.8 select_reduce_fusion.4
  10.3 0.6 gather_fusion
  11.0 0.0 copy-done.3
  11.0 0.1 compare_and_fusion
  11.1 0.7 fusion.9
  14.3 0.0 copy-done.4
  14.3 0.1 fusion.1
  14.4 72.8 %all-gather.3.cloned.1.call-done = f32[1024,1024]{0,1:T(8,128)} async-done(((f32[128,1024]{0,1:T(8,128)}), f32[1024,1024]{0,1:T(8,128)}) %all-gather.3.cloned.1.call-update) | async-done | bytes 4194320 | tf_op jit(solution)/shard_map/all_gather | solution.py:36
  87.2 1.9 dynamic-slice_multiply_fusion
  89.1 0.0 all-gather.5.cloned.1.call-update
  89.1 0.0 reduce-scatter.2.cloned.1.call-start
  89.2 0.1 broadcast_bitcast_fusion
  89.3 20.8 %all-gather.5.cloned.1.call-done = f32[1024,512]{0,1:T(8,128)} async-done(((f32[1024,128]{0,1:T(8,128)}), f32[1024,512]{0,1:T(8,128)}) %all-gather.5.cloned.1.call-update) | async-done | bytes 2097168 | tf_op jit(solution)/shard_map/all_gather | solution.py:42
  110.0 2.9 %copy.13 = f32[1024,4,128]{2,0,1:T(8,128)} copy(f32[1024,4,128]{0,2,1:T(8,128)} %bitcast.13) | data formatting | bytes 4194304 | tf_op jit(solution)/shard_map/reshape | solution.py:43
  113.0 3.6 %gather_fusion.1 = f32[4,1024,128]{2,1,0:T(8,128)} fusion(f32[1024,4,128]{2,0,1:T(8,128)} %copy.13, s32[1024]{0:T(1024)S(1)} %pad_clamp_fusion), kind=kCustom, calls=%fused_computation.1 | custom fusion | bytes 4194320 | tf_op jit(solution)/shard_map/jit(_take)/gather | solution.py:44
  116.6 2.9 %copy.14 = f32[1024,4,128]{0,2,1:T(8,128)} copy(f32[1024,4,128]{2,0,1:T(8,128)} %bitcast.12) | data formatting | bytes 4194304 | tf_op jit(solution)/shard_map/jit(_take)/gather | solution.py:44
  119.5 1.8 bitcast_select_fusion
  121.3 0.0 copy-done
  121.3 8.4 %fusion.12 = f32[1024,1024]{1,0:T(8,128)} fusion(f32[1024,512]{0,1:T(8,128)S(1)} %bitcast_select_fusion, f32[512,1024]{1,0:T(8,128)S(1)} %copy-done), kind=kOutput, calls=%fused_computation.51 | convolution fusion | flops 6442450944 | bytes 8388608 | tf_op jit(solution)/shard_map/dot_general | solution.py:46
  129.7 0.0 reduce-scatter.2.cloned.1.call-update
  129.8 0.6 copy-done.2
  130.4 0.6 select_reduce_fusion
  131.1 0.0 copy-done.5
  131.1 0.1 select_reduce_fusion.3
  131.2 86.6 %reduce-scatter.2.cloned.1.call-done = f32[128,1024]{1,0:T(8,128)} async-done(((f32[1024,1024]{1,0:T(8,128)}), f32[128,1024]{1,0:T(8,128)}) %reduce-scatter.2.cloned.1.call-update) | async-done | bytes 524304 | tf_op jit(solution)/shard_map/reduce_scatter | solution.py:45
  217.8 2.0 subtract_divide_fusion
  (13 shorter events, 0.1 us)
Async XLA Ops:
  6.5 114.8 %copy-start = (f32[512,1024]{1,0:T(8,128)S(1)}, f32[512,1024]{1,0:T(8,128)}, u32[]{:S(2)}) copy-start(f32[512,1024]{1,0:T(8,128)} %param.9) | copy-start | bytes 6291460
  6.5 4.4 %copy-start.3 = (s32[32]{0:T(128)S(1)}, s32[32]{0:T(128)}, u32[]{:S(2)}) copy-start(s32[32]{0:T(128)} %param.15) | copy-start | bytes 388
  6.5 7.7 %copy-start.4 = (s32[32]{0:T(128)S(1)}, s32[32]{0:T(128)}, u32[]{:S(2)}) copy-start(s32[32]{0:T(128)} %param.13) | copy-start | bytes 388
  6.5 80.6 %all-gather.3.cloned.1.call-start = ((), (), s32[]{:S(2)}) async-start(), calls=%async_computation.1 | async-start | bytes 4718592 | tf_op jit(solution)/shard_map/all_gather | solution.py:36
  8.8 101.3 %all-gather.5.cloned.1.call-start = ((), (), s32[]{:S(2)}) async-start(), calls=%async_computation.2 | async-start | bytes 2621440 | tf_op jit(solution)/shard_map/all_gather | solution.py:42
  89.1 128.7 %reduce-scatter.2.cloned.1.call-start = ((), (), s32[]{:S(2)}) async-start(), calls=%async_computation.3 | async-start | bytes 4718592 | tf_op jit(solution)/shard_map/reduce_scatter | solution.py:45
  129.7 0.7 copy-start.2
  129.7 1.4 copy-start.5
  129.7 88.1 %copy-start.1 = (f32[128,1024]{1,0:T(8,128)S(1)}, f32[128,1024]{1,0:T(8,128)}, u32[]{:S(2)}) copy-start(f32[128,1024]{1,0:T(8,128)} %param.10) | copy-start | bytes 1572868
Sparse Core Ops, SparseCore 0:
  9.4 77.7 all-gather.2
  89.2 20.7 all-gather.4
  129.9 87.9 reduce-scatter.1
where the time goes:
time: 227 us; the launch traced here: 226 us
  waiting for transfers between devices  180 us (79%)
  between operations  15.7 us (7%)
  local copies, waits for them, and re-layouts  13 us (6%)
  other arithmetic  8.96 us (4%)
  matrix products  8.4 us (4%)
    reduce_scatter x1, waiting for transfers between devices, on_device(): lax.psum_scatter(jnp.dot(amplitudes, integrals, precision=lax.Precision.H...  86.6 us
    all_gather x1, waiting for transfers between devices, on_device(): all_rows = lax.all_gather(t2_stored, 'amp', axis=0, tiled=True)  72.8 us
    all_gather x1, waiting for transfers between devices, on_device(): collected = lax.all_gather(piece, 'int', axis=1, tiled=True)  20.8 us
    dot_general x1, matrix products, on_device(): jnp.dot(amplitudes, integrals, precision=lax.Precision.HIGHEST, preferred...  8.4 us
    gather x2, local copies, waits for them, and re-layouts, on_device(): jnp.take(stacked, holder, axis=1).reshape(collected.shape[0], owned * TILE)  6.51 us
  transfers between devices with their start and end apart: 3, of which 3 were waited for; matrix products, arithmetic and copies ran while one was open for 2% of the time, Pallas kernels for 0%

commit v1 on v0

v1 whole, which is shorter than its diff:
```python
import functools

import jax
import jax.numpy as jnp
from jax import lax
from jax.experimental import pallas as pl
from jax.experimental.pallas import tpu as pltpu
from jax.sharding import PartitionSpec as P

NO = 120
NV = 600
TILE = 128
WIDTH = 128
MESH = pl.DeviceIdType.MESH


def split_index(ids, size):
    quotient = ((ids.astype(jnp.float32) + 0.5) * (1.0 / size)).astype(jnp.int32)
    return quotient, ids - quotient * size


def halves(values):
    high = values.astype(jnp.bfloat16)
    return high, (values - high.astype(jnp.float32)).astype(jnp.bfloat16)


def kernel(
    n_amp, n_int,
    t2_order, int_order, blk_len, t2, own_b, driver, eps_occ, eps_vir, out,
    unit, gathered, a_high, a_low, other_b, partial, arrived, vir_sum,
    b_send, b_recv, u_send, u_recv, y_send, core_send, g_recv, r_send, r_recv,
):
    amp = lax.axis_index("amp")
    q = lax.axis_index("int")
    groups = n_amp // 2
    ys = n_int // 2
    g, h = amp // 2, amp % 2
    y, core = q // 2, q % 2
    rows = t2.shape[0]
    slots = t2.shape[1] // TILE
    owned = own_b.shape[0] // TILE
    chunks = own_b.shape[1] // WIDTH
    partner = (g * 2 + 1 - h, q)
    sibling = (amp, y * 2 + 1 - core)

    def member(group):
        return (group * 2 + h, q)

    peers = [partner, sibling]
    peers += [member((g + k) % groups) for k in range(1, groups)]
    peers += [(amp, (y + k) % ys * 2 + core) for k in range(1, ys)]
    barrier = pltpu.get_barrier_semaphore()
    for peer in peers:
        pl.semaphore_signal(barrier, inc=1, device_id=peer, device_id_type=MESH)
    pl.semaphore_wait(barrier, len(peers))

    def remote(src, dst, send, recv, peer):
        return pltpu.make_async_remote_copy(
            src_ref=src, dst_ref=dst, send_sem=send, recv_sem=recv, device_id=peer, device_id_type=MESH
        )

    def b_copy(c):
        cols = pl.ds(pl.multiple_of(c * WIDTH, WIDTH), WIDTH)
        return remote(own_b.at[:, cols], other_b.at[c], b_send.at[c], b_recv.at[c], partner)

    @pl.loop(0, chunks)
    def _(c):
        b_copy(c).start()

    lane = lax.broadcasted_iota(jnp.int32, (rows, TILE), 1)

    def u_copy(group):
        return remote(unit.at[group], gathered.at[q, g], u_send.at[group], u_recv.at[g], member(group))

    def u_arrival(group):
        return remote(unit.at[group], gathered.at[q, group], u_send.at[group], u_recv.at[group], member(group))

    stored = [t2_order[q * slots + k] for k in range(slots)]
    lengths = []
    for k in range(slots):
        length = jnp.int32(0)
        for b in range(n_amp * owned):
            length += (stored[k] == b).astype(jnp.int32) * blk_len[b]
        lengths.append(length)

    def build(group):
        for side in range(2):
            p = group * 2 + (h if side == 0 else 1 - h)
            wanted = [int_order[p * owned + j] for j in range(owned)]
            total = jnp.zeros((rows, TILE), jnp.float32)
            for k in range(slots):
                held = jnp.int32(0)
                for block in wanted:
                    held += (stored[k] == block).astype(jnp.int32)
                total = jnp.where(lane < held * lengths[k], t2[:, k * TILE:(k + 1) * TILE], total)
            unit[group, :, side * TILE:(side + 1) * TILE] = total

    for k in range(1, groups):
        group = (g + k) % groups
        build(group)
        u_copy(group).start()
    build(g)
    gathered[q, g] = unit[g]

    def y_copy(k, group):
        return remote(
            gathered.at[q, group], gathered.at[q, group], y_send.at[k, group], g_recv.at[q, group],
            (amp, (y + k) % ys * 2 + core),
        )

    def core_copy(row, group):
        return remote(
            gathered.at[row, group], gathered.at[row, group], core_send.at[row, group], g_recv.at[row, group], sibling
        )

    def arrival(row, group):
        return remote(
            gathered.at[row, group], gathered.at[row, group], core_send.at[row, group], g_recv.at[row, group], sibling
        )

    for k in range(groups):
        group = (g + k) % groups
        if k > 0:
            u_arrival(group).wait_recv()
        for m in range(1, ys):
            y_copy(m, group).start()
        core_copy(q, group).start()


    row_ids = amp * rows + lax.broadcasted_iota(jnp.int32, (rows, NO), 0)
    place = lax.broadcasted_iota(jnp.int32, (rows, NO), 1)
    first, second = split_index(row_ids, NO)
    occ = jnp.broadcast_to(eps_occ[...], (rows, NO))
    occ_first = jnp.sum(jnp.where(place == first, occ, 0.0), axis=1, keepdims=True)
    occ_second = jnp.sum(jnp.where(place == second, occ, 0.0), axis=1, keepdims=True)

    for k in range(groups):
        group = (g + k) % groups
        for m in range(1, ys):
            row = (y + m) % ys * 2 + core
            arrival(row, group).wait_recv()
            core_copy(row, group).start()
    for k in range(groups):
        group = (g + k) % groups
        for m in range(ys):
            arrival((y + m) % ys * 2 + 1 - core, group).wait_recv()
    for side in range(2):
        p = g * 2 + (h if side == 0 else 1 - h)
        for j in range(owned):
            block = int_order[p * owned + j]
            shares = []
            for source in range(n_int):
                share = jnp.int32(0)
                for k in range(slots):
                    share += (t2_order[source * slots + k] == block).astype(jnp.int32)
                shares.append(jnp.full((rows, TILE), share, jnp.int32) > 0)
            for group in range(groups):
                picked = jnp.zeros((rows, TILE), jnp.float32)
                for source in range(n_int):
                    piece = gathered[source, group, :, side * TILE:(side + 1) * TILE]
                    picked = jnp.where(shares[source], piece, picked)
                high, low = halves(picked)
                spot = (pl.ds(group * rows, rows), pl.ds((side * owned + j) * TILE, TILE))
                a_high[spot] = high
                a_low[spot] = low

    def forward_copy(c, d, slot, group):
        return remote(partial.at[c, d], arrived.at[c, slot], r_send.at[c, d], r_recv.at[c, slot], member(group))

    def take_in(c, d, slot):
        remote(
            partial.at[c, d], arrived.at[c, slot], r_send.at[c, d], r_recv.at[c, slot], partner
        ).wait_recv()
        partial[c, d] += arrived[c, slot]

    @pl.loop(0, chunks + groups - 1)
    def _(t):
        @pl.when(t < chunks)
        def _():
            cols = pl.ds(pl.multiple_of(t * WIDTH, WIDTH), WIDTH)
            b_copy(t).wait_recv()
            high, low = halves(jnp.concatenate([own_b[:, cols], other_b[t]], axis=0))
            dot = functools.partial(jnp.dot, preferred_element_type=jnp.float32)
            product = dot(a_low[...], high) + dot(a_high[...], low) + dot(a_high[...], high)
            partial[t] = product.reshape(groups, rows, WIDTH)

            col_ids = q * own_b.shape[1] + t * WIDTH + lax.broadcasted_iota(jnp.int32, (NV, WIDTH), 1)
            spot = lax.broadcasted_iota(jnp.int32, (NV, WIDTH), 0)
            around, first_vir = split_index(col_ids, NV)
            second_vir = split_index(3 * col_ids + around, NV)[1]
            picks = (spot == first_vir).astype(jnp.float32) + (spot == second_vir).astype(jnp.float32)
            vir_sum[t] = jnp.dot(
                jnp.broadcast_to(eps_vir[...], (8, NV)), picks,
                precision=lax.Precision.HIGHEST, preferred_element_type=jnp.float32,
            )

        right = t - g
        left = t - (groups - 1 - g)

        @pl.when((right >= 0) & (right < chunks))
        def _():
            for d in range(groups - 1, 0, -1):
                @pl.when(d > g)
                def _(d=d):
                    @pl.when(g > 0)
                    def _():
                        take_in(right, d, d)
                    forward_copy(right, d, d, g + 1).start()

        @pl.when((left >= 0) & (left < chunks))
        def _():
            for d in range(groups - 1):
                @pl.when(d < g)
                def _(d=d):
                    @pl.when(g < groups - 1)
                    def _():
                        take_in(left, d, d)
                    forward_copy(left, d, jnp.where(d == g - 1, groups, d), g - 1).start()

        done = t - (groups - 1)

        @pl.when(done >= 0)
        def _():
            @pl.when(g > 0)
            def _():
                take_in(done, g, g)

            @pl.when(g < groups - 1)
            def _():
                take_in(done, g, groups)
            cols = pl.ds(pl.multiple_of(done * WIDTH, WIDTH), WIDTH)
            length = blk_len[q * chunks + done]
            live = (lane < length).astype(jnp.float32)
            denominators = vir_sum[done, 0:1, :] - occ_first - occ_second
            out[:, cols] = (driver[:, cols] + partial[done, g]) * live / denominators

    @pl.loop(0, chunks)
    def _(c):
        b_copy(c).wait_send()
        for d in range(groups):
            @pl.when(d != g)
            def _(d=d):
                forward_copy(c, d, d, g).wait_send()
    for k in range(1, groups):
        u_copy((g + k) % groups).wait_send()
    for group in range(groups):
        for m in range(1, ys):
            y_copy(m, group).wait_send()
        for m in range(ys):
            core_copy((y + m) % ys * 2 + core, group).wait_send()


def solution(mesh):
    n_amp, n_int = mesh.shape["amp"], mesh.shape["int"]

    def on_device(t2_stored, integrals, driver, eps_occ, eps_vir, blk_len, t2_order, int_order):
        rows = t2_stored.shape[0]
        depth, cols = integrals.shape
        groups, ys, chunks = n_amp // 2, n_int // 2, cols // WIDTH
        smem = pl.BlockSpec(memory_space=pltpu.SMEM)
        vmem = pl.BlockSpec(memory_space=pltpu.VMEM)
        dma = pltpu.SemaphoreType.DMA
        return pl.pallas_call(
            functools.partial(kernel, n_amp, n_int),
            out_shape=jax.ShapeDtypeStruct((rows, cols), jnp.float32),
            in_specs=[smem] * 3 + [vmem] * 5,
            out_specs=vmem,
            scratch_shapes=[
                pltpu.VMEM((groups, rows, 2 * TILE), jnp.float32),
                pltpu.VMEM((n_int, groups, rows, 2 * TILE), jnp.float32),
                pltpu.VMEM((groups * rows, n_int * 2 * TILE), jnp.bfloat16),
                pltpu.VMEM((groups * rows, n_int * 2 * TILE), jnp.bfloat16),
                pltpu.VMEM((chunks, depth, WIDTH), jnp.float32),
                pltpu.VMEM((chunks, groups, rows, WIDTH), jnp.float32),
                pltpu.VMEM((chunks, groups + 1, rows, WIDTH), jnp.float32),
                pltpu.VMEM((chunks, 8, WIDTH), jnp.float32),
                dma((chunks,)),
                dma((chunks,)),
                dma((groups,)),
                dma((groups,)),
                dma((ys, groups)),
                dma((n_int, groups)),
                dma((n_int, groups)),
                dma((chunks, groups)),
                dma((chunks, groups + 1)),
            ],
            compiler_params=pltpu.CompilerParams(
                collective_id=0, has_side_effects=True, vmem_limit_bytes=60 * 2**20
            ),
            cost_estimate=pl.CostEstimate(flops=6 * rows * groups * depth * 2 * cols, bytes_accessed=2**23, transcendentals=0),
        )(
            t2_order, int_order, blk_len, t2_stored, integrals, driver,
            eps_occ.reshape(1, NO), eps_vir.reshape(1, NV),
        )

    placed = (P("amp", "int"), P("amp", "int"), P("amp", "int"), P(), P(), P(), P(), P())
    return jax.shard_map(on_device, mesh=mesh, in_specs=placed, out_specs=P("amp", "int"), check_vma=False)
```

time: 227 us -> 75.8 us (0.33)
  waiting for transfers between devices: 180 us -> 0 us
  Pallas kernels: 0 us -> 72.5 us
  between operations: 15.7 us -> 0.01 us
  local copies, waits for them, and re-layouts: 13 us -> 3.15 us
  other arithmetic: 8.96 us -> 0 us
  matrix products: 8.4 us -> 0 us
    all_gather x2 -> x0, waiting for transfers between devices: 93.6 us -> none  [the longest x1 72.8 us: on_device(): all_rows = lax.all_gather(t2_stored, 'amp', axis=0, tiled=True)]
    reduce_scatter x1 -> x0, waiting for transfers between devices: 86.6 us -> none  [on_device(): lax.psum_scatter(jnp.dot(amplitudes, integrals, precision=lax.Precision.H...]
    pallas_call x0 -> x1, Pallas kernels: none -> 72.5 us  [on_device(): pl.pallas_call(functools.partial(kernel, n_amp, n_int), out_shape=jax.Sha...]
    dot_general x1 -> x0, matrix products: 8.4 us -> none  [on_device(): jnp.dot(amplitudes, integrals, precision=lax.Precision.HIGHEST, preferred...]
    gather x3 -> x0, local copies, waits for them, and re-layouts: 7.15 us -> none  [the longest x2 6.51 us: on_device(): jnp.take(stacked, holder, axis=1).reshape(collected.shape[0], owned * TILE)]
    select_n x4 -> x0, other arithmetic: 2.57 us -> none  [the longest x1 1.8 us: on_device(): jnp.take(stacked, holder, axis=1).reshape(collected.shape[0], owned * TILE)]
  transfers between devices with their start and end apart: 3 -> 0, of which waited for: 3 -> 0; matrix products, arithmetic and copies ran while one was open for 2% -> 0% of each run, Pallas kernels for 0% -> 0%
where the time goes in v1:
time: 75.8 us; the launch traced here: 75.6 us
  Pallas kernels  72.5 us (96%)
  local copies, waits for them, and re-layouts  3.15 us (4%)
    pallas_call x1, Pallas kernels, on_device(): pl.pallas_call(functools.partial(kernel, n_amp, n_int), out_shape=jax.Sha...  72.5 us
    unnamed x1, local copies, waits for them, and re-layouts  1.89 us

profile of v1, /device:TPU:0, one launch (start us, length us, event | category | flops | bytes accessed | tf_op | source)
XLA Modules:
  0.0 75.6 jit_solution(14765435404655763258)
XLA Ops:
  0.0 1.3 %reshape.7.eps_vir = f32[1,600]{1,0:T(1,128)} reshape(f32[600]{0:T(1024)} %param.12) | data formatting | bytes 4800 | tf_op jit(solution)/shard_map/reshape | solution.py:293
  1.3 72.5 %shard_map.82 = f32[128,1024]{1,0:T(8,128)} custom-call(s32[32]{0:T(128)} %t2_order.1, s32[32]{0:T(128)} %int_order.1, s32[32]{0:T(128)} %blk_len.1, f32[128,1024]{1,0:T(8,128)} %t2.1, f32[512,1024]{1,0:T(8,128)} %own_b.1, f32[128,1024]{1,0:T(8,128)} %driver.1, f32[1,120]{1,0:T(1,128)} %bitcast.1, f32[1,600]{1,0:T(1,128)} %reshape.7.eps_vir), custom_call_target="tpu_custom_call" | custom-call | flops 3221225472 | bytes 8388608 | tf_op jit(solution)/shard_map/pallas_call | solution.py:263
  73.7 1.9 %copy.10 = f32[128,1024]{1,0:T(8,128)} copy(f32[128,1024]{1,0:T(8,128)} %shard_map.82) | data formatting | bytes 1048576

commit v2 on v1

--- a/solution.py
+++ b/solution.py
@@ -134,35 +134,50 @@
     occ_first = jnp.sum(jnp.where(place == first, occ, 0.0), axis=1, keepdims=True)
     occ_second = jnp.sum(jnp.where(place == second, occ, 0.0), axis=1, keepdims=True)
 
+    @pl.loop(0, chunks)
+    def _(t):
+        col_ids = q * own_b.shape[1] + t * WIDTH + lax.broadcasted_iota(jnp.int32, (NV, WIDTH), 1)
+        spot = lax.broadcasted_iota(jnp.int32, (NV, WIDTH), 0)
+        around, first_vir = split_index(col_ids, NV)
+        second_vir = split_index(3 * col_ids + around, NV)[1]
+        picks = (spot == first_vir).astype(jnp.float32) + (spot == second_vir).astype(jnp.float32)
+        vir_sum[t] = jnp.dot(
+            jnp.broadcast_to(eps_vir[...].reshape(1, NV), (8, NV)), picks,
+            precision=lax.Precision.HIGHEST, preferred_element_type=jnp.float32,
+        )
+
     for k in range(groups):
         group = (g + k) % groups
         for m in range(1, ys):
             row = (y + m) % ys * 2 + core
             arrival(row, group).wait_recv()
             core_copy(row, group).start()
+    shares = []
+    for side in range(2):
+        p = g * 2 + (h if side == 0 else 1 - h)
+        for j in range(owned):
+            block = int_order[p * owned + j]
+            found = []
+            for source in range(n_int):
+                share = jnp.int32(0)
+                for k in range(slots):
+                    share += (t2_order[source * slots + k] == block).astype(jnp.int32)
+                found.append(share)
+            shares.append(found)
     for k in range(groups):
         group = (g + k) % groups
         for m in range(ys):
             arrival((y + m) % ys * 2 + 1 - core, group).wait_recv()
-    for side in range(2):
-        p = g * 2 + (h if side == 0 else 1 - h)
-        for j in range(owned):
-            block = int_order[p * owned + j]
-            shares = []
+        for place_of, found in enumerate(shares):
+            side = place_of // owned
+            picked = jnp.zeros((rows, TILE), jnp.float32)
             for source in range(n_int):
-                share = jnp.int32(0)
-                for k in range(slots):
-                    share += (t2_order[source * slots + k] == block).astype(jnp.int32)
-                shares.append(jnp.full((rows, TILE), share, jnp.int32) > 0)
-            for group in range(groups):
-                picked = jnp.zeros((rows, TILE), jnp.float32)
-                for source in range(n_int):
-                    piece = gathered[source, group, :, side * TILE:(side + 1) * TILE]
-                    picked = jnp.where(shares[source], piece, picked)
-                high, low = halves(picked)
-                spot = (pl.ds(group * rows, rows), pl.ds((side * owned + j) * TILE, TILE))
-                a_high[spot] = high
-                a_low[spot] = low
+                piece = gathered[source, group, :, side * TILE:(side + 1) * TILE]
+                picked = jnp.where(jnp.full((rows, TILE), found[source], jnp.int32) > 0, piece, picked)
+            high, low = halves(picked)
+            spot = (pl.ds(pl.multiple_of(group * rows, rows), rows), pl.ds(place_of * TILE, TILE))
+            a_high[spot] = high
+            a_low[spot] = low
 
     def forward_copy(c, d, slot, group):
         return remote(partial.at[c, d], arrived.at[c, slot], r_send.at[c, d], r_recv.at[c, slot], member(group))
@@ -183,16 +198,6 @@
             dot = functools.partial(jnp.dot, preferred_element_type=jnp.float32)
             product = dot(a_low[...], high) + dot(a_high[...], low) + dot(a_high[...], high)
             partial[t] = product.reshape(groups, rows, WIDTH)
-
-            col_ids = q * own_b.shape[1] + t * WIDTH + lax.broadcasted_iota(jnp.int32, (NV, WIDTH), 1)
-            spot = lax.broadcasted_iota(jnp.int32, (NV, WIDTH), 0)
-            around, first_vir = split_index(col_ids, NV)
-            second_vir = split_index(3 * col_ids + around, NV)[1]
-            picks = (spot == first_vir).astype(jnp.float32) + (spot == second_vir).astype(jnp.float32)
-            vir_sum[t] = jnp.dot(
-                jnp.broadcast_to(eps_vir[...], (8, NV)), picks,
-                precision=lax.Precision.HIGHEST, preferred_element_type=jnp.float32,
-            )
 
         right = t - g
         left = t - (groups - 1 - g)
@@ -290,7 +295,7 @@
             cost_estimate=pl.CostEstimate(flops=6 * rows * groups * depth * 2 * cols, bytes_accessed=2**23, transcendentals=0),
         )(
             t2_order, int_order, blk_len, t2_stored, integrals, driver,
-            eps_occ.reshape(1, NO), eps_vir.reshape(1, NV),
+            eps_occ.reshape(1, NO), eps_vir,
         )
 
     placed = (P("amp", "int"), P("amp", "int"), P("amp", "int"), P(), P(), P(), P(), P())

time: 75.8 us -> 74.6 us (0.984)
  local copies, waits for them, and re-layouts: 3.15 us -> 1.89 us
    reshape x1 -> x0, local copies, waits for them, and re-layouts: 1.27 us -> none  [on_device(): eps_vir.reshape(1, NV)]
where the time goes in v2:
time: 74.6 us; the launch traced here: 74.5 us
  Pallas kernels  72.6 us (97%)
  local copies, waits for them, and re-layouts  1.89 us (3%)
    pallas_call x1, Pallas kernels, on_device(): pl.pallas_call(functools.partial(kernel, n_amp, n_int), out_shape=jax.Sha...  72.6 us
    unnamed x1, local copies, waits for them, and re-layouts  1.89 us

profile of v2, /device:TPU:0, one launch (start us, length us, event | category | flops | bytes accessed | tf_op | source)
XLA Modules:
  0.0 74.5 jit_solution(1650685653944689780)
XLA Ops:
  0.0 72.6 %shard_map.82 = f32[128,1024]{1,0:T(8,128)} custom-call(s32[32]{0:T(128)} %t2_order.1, s32[32]{0:T(128)} %int_order.1, s32[32]{0:T(128)} %blk_len.1, f32[128,1024]{1,0:T(8,128)} %t2.1, f32[512,1024]{1,0:T(8,128)} %own_b.1, f32[128,1024]{1,0:T(8,128)} %driver.1, f32[1,120]{1,0:T(1,128)} %bitcast.1, f32[600]{0:T(1024)} %eps_vir.1), custom_call_target="tpu_custom_call" | custom-call | flops 3221225472 | bytes 8388608 | tf_op jit(solution)/shard_map/pallas_call | solution.py:268
  72.6 1.9 %copy.10 = f32[128,1024]{1,0:T(8,128)} copy(f32[128,1024]{1,0:T(8,128)} %shard_map.82) | data formatting | bytes 1048576

commit v3 on v2

--- a/solution.py
+++ b/solution.py
@@ -10,7 +10,7 @@
 NO = 120
 NV = 600
 TILE = 128
-WIDTH = 128
+WIDTH = 256
 MESH = pl.DeviceIdType.MESH
 
 
@@ -234,8 +234,10 @@
             def _():
                 take_in(done, g, groups)
             cols = pl.ds(pl.multiple_of(done * WIDTH, WIDTH), WIDTH)
-            length = blk_len[q * chunks + done]
-            live = (lane < length).astype(jnp.float32)
+            tiles = WIDTH // TILE
+            live = jnp.concatenate(
+                [(lane < blk_len[(q * chunks + done) * tiles + i]).astype(jnp.float32) for i in range(tiles)], axis=1
+            )
             denominators = vir_sum[done, 0:1, :] - occ_first - occ_second
             out[:, cols] = (driver[:, cols] + partial[done, g]) * live / denominators
 

time: 74.6 us -> 73.9 us (level)
  no operation moved by 1% of the time
where the time goes in v3:
time: 73.9 us; the launch traced here: 73.8 us
  Pallas kernels  71.9 us (97%)
  local copies, waits for them, and re-layouts  1.89 us (3%)
    pallas_call x1, Pallas kernels, on_device(): pl.pallas_call(functools.partial(kernel, n_amp, n_int), out_shape=jax.Sha...  71.9 us
    unnamed x1, local copies, waits for them, and re-layouts  1.89 us

profile of v3, /device:TPU:0, one launch (start us, length us, event | category | flops | bytes accessed | tf_op | source)
XLA Modules:
  0.0 73.8 jit_solution(6091533131837449877)
XLA Ops:
  0.0 71.9 %shard_map.82 = f32[128,1024]{1,0:T(8,128)} custom-call(s32[32]{0:T(128)} %t2_order.1, s32[32]{0:T(128)} %int_order.1, s32[32]{0:T(128)} %blk_len.1, f32[128,1024]{1,0:T(8,128)} %t2.1, f32[512,1024]{1,0:T(8,128)} %own_b.1, f32[128,1024]{1,0:T(8,128)} %driver.1, f32[1,120]{1,0:T(1,128)} %bitcast.1, f32[600]{0:T(1024)} %eps_vir.1), custom_call_target="tpu_custom_call" | custom-call | flops 3221225472 | bytes 8388608 | tf_op jit(solution)/shard_map/pallas_call | solution.py:270
  71.9 1.9 %copy.10 = f32[128,1024]{1,0:T(8,128)} copy(f32[128,1024]{1,0:T(8,128)} %shard_map.82) | data formatting | bytes 1048576

commit v4 on v3

--- a/solution.py
+++ b/solution.py
@@ -190,6 +190,25 @@
 
     @pl.loop(0, chunks + groups - 1)
     def _(t):
+        right = t - g
+        left = t - (groups - 1 - g)
+
+        @pl.when((g > 0) & (right >= 0) & (right < chunks))
+        def _():
+            for d in range(groups - 1, 0, -1):
+                @pl.when(d > g)
+                def _(d=d):
+                    take_in(right, d, d)
+                    forward_copy(right, d, d, g + 1).start()
+
+        @pl.when((g < groups - 1) & (left >= 0) & (left < chunks))
+        def _():
+            for d in range(groups - 1):
+                @pl.when(d < g)
+                def _(d=d):
+                    take_in(left, d, d)
+                    forward_copy(left, d, jnp.where(d == g - 1, groups, d), g - 1).start()
+
         @pl.when(t < chunks)
         def _():
             cols = pl.ds(pl.multiple_of(t * WIDTH, WIDTH), WIDTH)
@@ -199,28 +218,15 @@
             product = dot(a_low[...], high) + dot(a_high[...], low) + dot(a_high[...], high)
             partial[t] = product.reshape(groups, rows, WIDTH)
 
-        right = t - g
-        left = t - (groups - 1 - g)
-
-        @pl.when((right >= 0) & (right < chunks))
+        @pl.when((g == 0) & (t < chunks))
         def _():
             for d in range(groups - 1, 0, -1):
-                @pl.when(d > g)
-                def _(d=d):
-                    @pl.when(g > 0)
-                    def _():
-                        take_in(right, d, d)
-                    forward_copy(right, d, d, g + 1).start()
-
-        @pl.when((left >= 0) & (left < chunks))
+                forward_copy(t, d, d, 1).start()
+
+        @pl.when((g == groups - 1) & (t < chunks))
         def _():
             for d in range(groups - 1):
-                @pl.when(d < g)
-                def _(d=d):
-                    @pl.when(g < groups - 1)
-                    def _():
-                        take_in(left, d, d)
-                    forward_copy(left, d, jnp.where(d == g - 1, groups, d), g - 1).start()
+                forward_copy(t, d, groups if d == groups - 2 else d, groups - 2).start()
 
         done = t - (groups - 1)
 

time: 73.9 us -> 73.9 us (level)
  no operation moved by 1% of the time
where the time goes in v4:
time: 73.9 us; the launch traced here: 73.8 us
  Pallas kernels  71.9 us (97%)
  local copies, waits for them, and re-layouts  1.89 us (3%)
    pallas_call x1, Pallas kernels, on_device(): pl.pallas_call(functools.partial(kernel, n_amp, n_int), out_shape=jax.Sha...  71.9 us
    unnamed x1, local copies, waits for them, and re-layouts  1.89 us

profile of v4, /device:TPU:0, one launch (start us, length us, event | category | flops | bytes accessed | tf_op | source)
XLA Modules:
  0.0 73.8 jit_solution(10553609273804087751)
XLA Ops:
  0.0 71.9 %shard_map.82 = f32[128,1024]{1,0:T(8,128)} custom-call(s32[32]{0:T(128)} %t2_order.1, s32[32]{0:T(128)} %int_order.1, s32[32]{0:T(128)} %blk_len.1, f32[128,1024]{1,0:T(8,128)} %t2.1, f32[512,1024]{1,0:T(8,128)} %own_b.1, f32[128,1024]{1,0:T(8,128)} %driver.1, f32[1,120]{1,0:T(1,128)} %bitcast.1, f32[600]{0:T(1024)} %eps_vir.1), custom_call_target="tpu_custom_call" | custom-call | flops 3221225472 | bytes 8388608 | tf_op jit(solution)/shard_map/pallas_call | solution.py:276
  71.9 1.9 %copy.10 = f32[128,1024]{1,0:T(8,128)} copy(f32[128,1024]{1,0:T(8,128)} %shard_map.82) | data formatting | bytes 1048576
